TPU v7x, 128 devices: a whole 4x4x4 slice. The times are simulated.
128 devices in a mesh: expert: 4 (over y), feat: 32 (over x, z, core).
Axes of the slice: x: 4, y: 4, z: 4, core: 2. Of those that a mesh axis runs over, the one named last changes fastest.
Arguments:
- tokens: bfloat16 [1024, 4096], P(('expert', 'feat')), may hold values from -6 to 6
- expert_ids: int32 [1024, 2], P(('expert', 'feat')), may hold values from 0 to 7, as said below
- route_weights: bfloat16 [1024, 2], P(('expert', 'feat')), may hold values from 0.099609375 to 1
- gate_proj: bfloat16 [4096, 28672], P(None, ('expert', 'feat')), may hold values from -0.09375 to 0.09375
- up_proj: bfloat16 [4096, 28672], P(None, ('expert', 'feat')), may hold values from -0.09375 to 0.09375
- down_proj: bfloat16 [28672, 4096], P(('expert', 'feat')), may hold values from -0.046875 to 0.046875
- enc_weight: float32 [4096, 32768], P(None, ('expert', 'feat')), may hold values from -0.09375 to 0.09375
- enc_bias: float32 [32768], P(('expert', 'feat')), may hold values from -3 to 3
- log_threshold: float32 [32768], P(('expert', 'feat')), may hold values from -2.3 to 0
- dec_weight: float32 [32768, 4096], P(('expert', 'feat')), may hold values from -0.046875 to 0.046875
Outputs:
- grad_encoder: float32 [4096, 32768], P(None, ('expert', 'feat'))
- grad_decoder: float32 [32768, 4096], P(('expert', 'feat'))
- grad_bias: float32 [32768], P(('expert', 'feat'))
- grad_threshold: float32 [32768], P(('expert', 'feat'))
Inputs may be any that keep to these rules, and one draw needn't show every extreme that they name: `expert_ids`: each token names two different experts of 0 to 7. Among the 8 tokens of one device, each expert below 2 is named by at most 4 tokens; in every draw one of these experts, drawn from the seed and the same for all devices, is named by exactly 4 tokens of every device.
All inputs are finite; a program needn't handle non-finite values.
Results may differ from a plain program's by a relative error of at most 0.0021.
Values may be sent and summed in bfloat16 or wider, within the bound.
A program may use at most 128 MiB of HBM per device.

v0:
```python
import jax
import jax.numpy as jnp
from jax import lax
from jax.sharding import PartitionSpec as P

sharpness = 0.1
kernel_width = 0.5
density_weight = 0.01
highest = lax.Precision.HIGHEST


def partner(block, axis, stride):
    count = lax.axis_size(axis)
    route = []
    for low in range(count):
        high = low | 1 << stride
        if high != low and high < count:
            route += [(low, high), (high, low)]
    return lax.ppermute(block, axis, route)


def pack_slots(tokens, expert_ids, route_weights, experts):
    capacity = tokens.shape[0] // 2
    window = jnp.arange(experts, dtype=jnp.int32)
    matches = expert_ids[:, :, None] == window[None, None, :]
    named = jnp.sum(matches.astype(jnp.int32), axis=1)
    weighted = jnp.sum(
        jnp.where(matches, route_weights[:, :, None], jnp.zeros((), jnp.bfloat16)), axis=1
    )
    slot_index = jnp.cumsum(named, axis=0) - named
    places = jnp.arange(capacity, dtype=jnp.int32)
    chosen = (named.T[:, None, :] == 1) & (slot_index.T[:, None, :] == places[None, :, None])
    slot_rows = jnp.einsum(
        "ect,td->ecd", chosen.astype(jnp.bfloat16), tokens, preferred_element_type=jnp.float32
    ).astype(jnp.bfloat16)
    slot_weights = jnp.sum(
        jnp.where(chosen, weighted.T[:, None, :], jnp.zeros((), jnp.bfloat16)), axis=2
    )
    return (slot_rows, slot_weights)


def contract_rows(left, right):
    return lax.dot_general(left, right, (((0,), (0,)), ((), ())), precision=highest)


def body(
    tokens,
    expert_ids,
    route_weights,
    gate_proj,
    up_proj,
    down_proj,
    enc_weight,
    enc_bias,
    log_threshold,
    dec_weight,
):
    copies = 2
    experts = lax.axis_size("expert") // copies
    slot_rows, slot_weights = pack_slots(tokens, expert_ids, route_weights, experts)
    send_rows = jnp.repeat(slot_rows, copies, axis=0)
    send_weights = jnp.repeat(slot_weights, copies, axis=0)
    came_rows, came_weights = (
        lax.all_to_all(send_rows, "expert", split_axis=0, concat_axis=0, tiled=True),
        lax.all_to_all(send_weights, "expert", split_axis=0, concat_axis=0, tiled=True),
    )
    all_rows, all_weights = (
        lax.all_gather(came_rows, "feat", axis=0, tiled=True),
        lax.all_gather(came_weights, "feat", axis=0, tiled=True),
    )
    width = tokens.shape[1]
    token_rows = all_rows.reshape(-1, width)
    row_weights = all_weights.reshape(-1).astype(jnp.float32)
    gate_act = jnp.dot(token_rows, gate_proj, preferred_element_type=jnp.float32)
    up_act = jnp.dot(token_rows, up_proj, preferred_element_type=jnp.float32)
    hidden = (jax.nn.silu(gate_act) * up_act).astype(jnp.bfloat16)
    target_part = jnp.dot(hidden, down_proj, preferred_element_type=jnp.float32)
    inputs = token_rows.astype(jnp.float32)
    preact = jnp.dot(inputs, enc_weight, precision=highest) + enc_bias
    threshold = jnp.exp(log_threshold)
    shifted = preact - threshold
    soft_gate = jax.nn.sigmoid(shifted / sharpness)
    active = preact * soft_gate
    partial_error = jnp.dot(active, dec_weight, precision=highest) - target_part
    feat_total = lax.psum(partial_error, "feat")
    recon_error = feat_total + partner(feat_total, "expert", 0)
    residual_grad = 2.0 * row_weights[:, None] * recon_error
    grad_decoder = contract_rows(active, residual_grad)
    grad_active = lax.dot_general(
        residual_grad, dec_weight, (((1,), (1,)), ((), ())), precision=highest
    )
    grad_pre = grad_active * soft_gate
    grad_encoder = contract_rows(inputs, grad_pre)
    grad_bias = jnp.sum(grad_pre, axis=0)
    kernel = jnp.maximum(0.0, 1.0 - jnp.abs(shifted) / kernel_width) / kernel_width
    slope_sum = jnp.sum(
        (grad_active * threshold + density_weight * row_weights[:, None]) * kernel, axis=0
    )
    grad_threshold = -threshold * slope_sum
    return (grad_encoder, grad_decoder, grad_bias, grad_threshold)


def solution(mesh):
    in_specs = (
        P(("expert", "feat"), None),
        P(("expert", "feat"), None),
        P(("expert", "feat"), None),
        P(None, ("expert", "feat")),
        P(None, ("expert", "feat")),
        P(("expert", "feat"), None),
        P(None, ("expert", "feat")),
        P(("expert", "feat")),
        P(("expert", "feat")),
        P(("expert", "feat"), None),
    )
    out_specs = (
        P(None, ("expert", "feat")),
        P(("expert", "feat"), None),
        P(("expert", "feat")),
        P(("expert", "feat")),
    )
    return jax.shard_map(body, mesh=mesh, in_specs=in_specs, out_specs=out_specs, check_vma=False)
```

profile of v0, /device:TPU:1, one launch (start us, length us, event | category | flops | bytes accessed | tf_op | source)
XLA Modules:
  0.0 474.6 jit_solution(3377354966974964132)
XLA Ops:
  7.2 0.0 copy-start
  7.2 0.0 all-gather.3.cloned.1.call-start
  7.2 0.8 convert_reduce_fusion
  8.1 0.2 reduce_window_sum.11
  8.2 1.0 convolution_convert_fusion
  9.3 9.7 %all_to_all.17 = bf16[4,4,4096]{2,1,0:T(4,128)(2,1)} all-to-all(bf16[4,4,4096]{2,1,0:T(4,128)(2,1)S(1)} %bitcast.20), channel_id=1, replica_groups=mesh['expert'=4,'feat'=32] {'expert'}, dimensions={0} | all-to-all | bytes 262144 | tf_op jit(solution)/shard_map/all_to_all | solution.py:64
  19.0 0.0 all-gather.3.cloned.1.call-update
  19.0 0.0 all-reduce.2.cloned.1.call-start
  19.1 0.7 exp.10
  19.8 48.0 %all-gather.3.cloned.1.call-done = bf16[128,4,4096]{2,1,0:T(4,128)(2,1)} async-done(((bf16[4,4,4096]{2,1,0:T(4,128)(2,1)}), bf16[128,4,4096]{2,1,0:T(4,128)(2,1)}) %all-gather.3.cloned.1.call-update) | async-done | bytes 4194320 | tf_op jit(solution)/shard_map/all_gather | solution.py:68
  67.8 6.9 %reshape.45 = bf16[512,4096]{1,0:T(8,128)(2,1)} reshape(bf16[128,4,4096]{2,1,0:T(4,128)(2,1)} %all-gather.3.cloned.1.call-done) | data formatting | bytes 8388608 | tf_op jit(solution)/shard_map/reshape | solution.py:72
  74.7 0.0 copy-start.1
  74.7 0.0 copy-start.7
  74.7 4.3 fusion.31
  79.0 0.0 copy-done.1
  79.0 0.0 copy-done.7
  79.0 5.8 %convolution_add_fusion = f32[512,256]{1,0:T(8,128)S(1)} fusion(bf16[512,4096]{1,0:T(8,128)(2,1)S(1)} %copy-done.1, f32[4096,256]{1,0:T(8,128)} %param.16, f32[256]{0:T(256)S(1)} %copy-done.7), kind=kOutput, calls=%fused_computation.6 | convolution fusion | flops 6442582016 | bytes 8913920 | tf_op jit(solution)/shard_map/dot_general | solution.py:79
  84.9 0.0 copy-done
  84.9 8.7 %fusion.3 = f32[512,4096]{1,0:T(8,128)} fusion(bf16[224,4096]{1,0:T(8,128)(2,1)S(1)} %copy-done, bf16[512,4096]{1,0:T(8,128)(2,1)} %reshape.45, bf16[4096,224]{0,1:T(8,128)(2,1)} %param.14, f32[512,224]{0,1:T(8,128)S(1)} %fusion.31), kind=kOutput, calls=%fused_computation.8 | convolution fusion | flops 1879736320 | bytes 16711680 | tf_op jit(solution)/shard_map/dot_general | solution.py:77
  93.6 13.0 %convolution_subtract_fusion = f32[512,4096]{1,0:T(8,128)} fusion(f32[512,4096]{1,0:T(8,128)} %fusion.3, f32[256,4096]{1,0:T(8,128)} %param.19, f32[512,256]{1,0:T(8,128)S(1)} %convolution_add_fusion, f32[256]{0:T(256)S(1)} %exp.10), kind=kOutput, calls=%fused_computation.1 | convolution fusion | flops 6445334528 | bytes 21496832 | tf_op jit(solution)/shard_map/dot_general | solution.py:84
  106.6 0.0 copy-start.5
  106.6 0.0 copy-start.6
  106.6 0.0 all-reduce.2.cloned.1.call-update
  106.6 119.7 %all-reduce.2.cloned.1.call-done = f32[512,4096]{1,0:T(8,128)} async-done(((f32[512,4096]{1,0:T(8,128)}), f32[512,4096]{1,0:T(8,128)}) %all-reduce.2.cloned.1.call-update) | async-done | bytes 8388624 | tf_op jit(solution)/shard_map/psum | solution.py:85
  226.4 1.2 collective-permute-start
  227.6 0.0 copy-done.5
  227.6 0.0 copy-done.6
  227.6 0.1 fusion.18
  227.7 181.8 %all_to_all.18 = bf16[4,1,4]{2,1,0:T(2,128)(2,1)S(1)} all-to-all(bf16[4,1,4]{2,1,0:T(2,128)(2,1)S(1)} %copy.21), channel_id=1, replica_groups=mesh['expert'=4,'feat'=32] {'expert'}, dimensions={0} | all-to-all | bytes 64 | tf_op jit(solution)/shard_map/all_to_all | solution.py:65
  409.5 26.1 %all-gather = bf16[128,1,4]{2,1,0:T(2,128)(2,1)S(1)} all-gather(bf16[4,1,4]{2,1,0:T(2,128)(2,1)S(1)} %all_to_all.18), channel_id=2, replica_groups=mesh['expert'=4,'feat'=32] {'feat'}, dimensions={0}, use_global_device_ids=true | all-gather | bytes 1056 | tf_op jit(solution)/shard_map/all_gather | solution.py:69
  435.6 0.4 multiply_reduce_fusion.1
  436.0 0.1 mul.73
  436.1 0.1 mul.63
  436.2 0.0 copy-start.2
  436.2 0.0 collective-permute-done
  436.2 13.2 %multiply_reduce_fusion = (f32[256]{0:T(256)S(1)}, f32[256]{0:T(256)}, f32[512,256]{1,0:T(8,128)S(1)}) fusion(f32[512,256]{1,0:T(8,128)S(1)} %convolution_add_fusion, f32[512]{0:T(512)S(1)} %mul.73, f32[256]{0:T(256)S(1)} %exp.10, f32[256,4096]{1,0:T(8,128)} %param.19, f32[512,4096]{1,0:T(8,128)} %all-reduce.2.cloned.1.call-done, ...), kind=kOutput, calls=%fused_computation.9 | convolution fusion | flops 6448741888 | bytes 22027264 | tf_op jit(solution)/shard_map/dot_general | solution.py:89
  449.4 0.0 copy-done.2
  449.4 0.0 copy-start.4
  449.4 0.0 copy-start.3
  449.4 6.3 %fusion.29 = f32[4096,256]{1,0:T(8,128)} fusion(bf16[512,4096]{1,0:T(8,128)(2,1)S(1)} %copy-done.2, f32[512,256]{1,0:T(8,128)S(1)} %get-tuple-element.8, f32[512,256]{1,0:T(8,128)S(1)} %convolution_add_fusion, f32[256]{0:T(256)S(1)} %exp.10), kind=kOutput, calls=%fused_computation.41 | convolution fusion | flops 6443237376 | bytes 9438208 | tf_op jit(solution)/shard_map/dot_general | solution.py:43
  455.7 0.0 copy-done.4
  455.7 0.6 negate_multiply_fusion
  456.3 0.0 copy-done.3
  456.3 11.5 %fusion = f32[256,4096]{1,0:T(8,128)} fusion(f32[512,4096]{1,0:T(8,128)S(1)} %copy-done.3, f32[512,4096]{1,0:T(8,128)} %collective-permute-done, f32[512]{0:T(512)S(1)} %mul.63, f32[512,256]{1,0:T(8,128)S(1)} %convolution_add_fusion, f32[256]{0:T(256)S(1)} %exp.10), kind=kOutput, calls=%fused_computation.4 | convolution fusion | flops 6447431680 | bytes 21498880 | tf_op jit(solution)/shard_map/dot_general | solution.py:43
  (6 shorter events, 0.1 us)
Async XLA Ops:
  7.2 77.7 %copy-start = (bf16[224,4096]{1,0:T(8,128)(2,1)S(1)}, bf16[224,4096]{1,0:T(8,128)(2,1)}, u32[]{:S(2)}) copy-start(bf16[224,4096]{1,0:T(8,128)(2,1)} %param.15) | copy-start | bytes 5505028
  7.2 60.6 %all-gather.3.cloned.1.call-start = ((), (), s32[]{:S(2)}) async-start(), calls=%async_computation.2 | async-start | bytes 4325376 | tf_op jit(solution)/shard_map/all_gather | solution.py:68
  19.0 207.3 %all-reduce.2.cloned.1.call-start = ((), (), s32[]{:S(2)}) async-start(), calls=%async_computation.3 | async-start | bytes 16777216 | tf_op jit(solution)/shard_map/psum | solution.py:85
  74.7 4.4 copy-start.1
  74.7 4.4 copy-start.7
  106.6 121.0 %copy-start.5 = (s32[8,2]{0,1:T(2,128)S(1)}, s32[8,2]{0,1:T(2,128)}, u32[]{:S(2)}) copy-start(s32[8,2]{0,1:T(2,128)} %param.11) | copy-start | bytes 196
  106.6 121.0 %copy-start.6 = (bf16[8,2]{0,1:T(2,128)(2,1)S(1)}, bf16[8,2]{0,1:T(2,128)(2,1)}, u32[]{:S(2)}) copy-start(bf16[8,2]{0,1:T(2,128)(2,1)} %param.12) | copy-start | bytes 100
  226.4 209.8 %collective-permute-start = (f32[512,4096]{1,0:T(8,128)}, f32[512,4096]{1,0:T(8,128)}, u32[]{:S(2)}, u32[]{:S(2)}) collective-permute-start(f32[512,4096]{1,0:T(8,128)} %all-reduce.2.cloned.1.call-done), channel_id=1, source_target_pairs={{0,32},{32,0},{64,96},{96,64},{1,33},{33,1},{65,97},{97,65},{2,34}... | collective-permute-start | bytes 25165832 | tf_op jit(solution)/shard_map/ppermute | solution.py:19
  436.2 13.2 %copy-start.2 = (bf16[512,4096]{1,0:T(8,128)(2,1)S(1)}, bf16[512,4096]{1,0:T(8,128)(2,1)}, u32[]{:S(2)}) copy-start(bf16[512,4096]{1,0:T(8,128)(2,1)} %reshape.45) | copy-start | bytes 12582916
  449.4 6.3 %copy-start.4 = (f32[256]{0:T(256)S(1)}, f32[256]{0:T(256)}, u32[]{:S(2)}) copy-start(f32[256]{0:T(256)} %param.18) | copy-start | bytes 3076
  449.4 6.9 %copy-start.3 = (f32[512,4096]{1,0:T(8,128)S(1)}, f32[512,4096]{1,0:T(8,128)}, u32[]{:S(2)}) copy-start(f32[512,4096]{1,0:T(8,128)} %all-reduce.2.cloned.1.call-done) | copy-start | bytes 25165828
Sparse Core Ops, SparseCore 0:
  19.2 48.5 all-gather.2
  106.8 119.5 all-reduce.1
where the time goes:
time: 475 us
  blocking collectives  218 us (46%)
  waiting for transfers between devices  168 us (35%)
  matrix products  63.9 us (13%)
  between operations  14.1 us (3%)
  local copies, waits for them, and re-layouts  7.86 us (2%)
    all_to_all x1, blocking collectives, body(): lax.all_to_all(send_weights, 'expert', split_axis=0, concat_axis=0, tiled...  182 us
    psum x1, waiting for transfers between devices, body(): feat_total = lax.psum(partial_error, 'feat')  120 us
    all_gather x1, waiting for transfers between devices, body(): lax.all_gather(came_rows, 'feat', axis=0, tiled=True)  48 us
    all_gather x1, blocking collectives, body(): lax.all_gather(came_weights, 'feat', axis=0, tiled=True)  26.1 us
    dot_general x2, matrix products, contract_rows(): lax.dot_general(left, right, (((0,), (0,)), ((), ())), precision=highest)  17.8 us
    dot_general x1, matrix products, body(): lax.dot_general(residual_grad, dec_weight, (((1,), (1,)), ((), ())), prec...  13.2 us
    dot_general x1, matrix products, body(): partial_error = jnp.dot(active, dec_weight, precision=highest) - target_part  13 us
    all_to_all x1, blocking collectives, body(): lax.all_to_all(send_rows, 'expert', split_axis=0, concat_axis=0, tiled=True)  9.75 us
  transfers between devices with their start and end apart: 3, of which 2 were waited for; matrix products, arithmetic and copies ran while one was open for 0% of the time, Pallas kernels for 0%

commit v1 on v0

--- a/solution.py
+++ b/solution.py
@@ -7,6 +7,11 @@
 kernel_width = 0.5
 density_weight = 0.01
 highest = lax.Precision.HIGHEST
+
+
+def gather_over(x, name, along):
+    sent = jnp.stack([x] * lax.axis_size(name))
+    return jnp.concatenate(lax.all_to_all(sent, name, 0, 0), axis=along)
 
 
 def partner(block, axis, stride):
@@ -66,7 +71,7 @@
     )
     all_rows, all_weights = (
         lax.all_gather(came_rows, "feat", axis=0, tiled=True),
-        lax.all_gather(came_weights, "feat", axis=0, tiled=True),
+        gather_over(came_weights, "feat", 0),
     )
     width = tokens.shape[1]
     token_rows = all_rows.reshape(-1, width)

time: 475 us -> 463 us (0.975)
  blocking collectives: 218 us -> 206 us
    all_gather x1 -> x0, blocking collectives: 26.1 us -> none  [body(): lax.all_gather(came_weights, 'feat', axis=0, tiled=True)]
    all_to_all x0 -> x1, blocking collectives: none -> 14.5 us  [gather_over(): return jnp.concatenate(lax.all_to_all(sent, name, 0, 0), axis=along)]
where the time goes in v1:
time: 463 us
  blocking collectives  206 us (44%)
  waiting for transfers between devices  168 us (36%)
  matrix products  63.9 us (14%)
  between operations  14.1 us (3%)
  local copies, waits for them, and re-layouts  7.9 us (2%)
    all_to_all x1, blocking collectives, body(): lax.all_to_all(send_weights, 'expert', split_axis=0, concat_axis=0, tiled...  182 us
    psum x1, waiting for transfers between devices, body(): feat_total = lax.psum(partial_error, 'feat')  120 us
    all_gather x1, waiting for transfers between devices, body(): lax.all_gather(came_rows, 'feat', axis=0, tiled=True)  48 us
    dot_general x2, matrix products, contract_rows(): lax.dot_general(left, right, (((0,), (0,)), ((), ())), precision=highest)  17.8 us
    all_to_all x1, blocking collectives, gather_over(): return jnp.concatenate(lax.all_to_all(sent, name, 0, 0), axis=along)  14.5 us
    dot_general x1, matrix products, body(): lax.dot_general(residual_grad, dec_weight, (((1,), (1,)), ((), ())), prec...  13.2 us
    dot_general x1, matrix products, body(): partial_error = jnp.dot(active, dec_weight, precision=highest) - target_part  13 us
    all_to_all x1, blocking collectives, body(): lax.all_to_all(send_rows, 'expert', split_axis=0, concat_axis=0, tiled=True)  9.75 us
  transfers between devices with their start and end apart: 3, of which 2 were waited for; matrix products, arithmetic and copies ran while one was open for 0% of the time, Pallas kernels for 0%

profile of v1, /device:TPU:1, one launch (start us, length us, event | category | flops | bytes accessed | tf_op | source)
XLA Modules:
  0.0 462.7 jit_solution(16110298809443467607)
XLA Ops:
  7.2 0.0 copy-start
  7.2 0.0 all-gather.2.cloned.1.call-start
  7.2 0.8 convert_reduce_fusion
  8.1 0.2 reduce_window_sum.11
  8.2 1.0 convolution_convert_fusion
  9.3 9.7 %all_to_all.19 = bf16[4,4,4096]{2,1,0:T(4,128)(2,1)} all-to-all(bf16[4,4,4096]{2,1,0:T(4,128)(2,1)S(1)} %bitcast.23), channel_id=1, replica_groups=mesh['expert'=4,'feat'=32] {'expert'}, dimensions={0} | all-to-all | bytes 262144 | tf_op jit(solution)/shard_map/all_to_all | solution.py:69
  19.0 0.0 all-gather.2.cloned.1.call-update
  19.0 0.0 all-reduce.2.cloned.1.call-start
  19.1 0.7 exp.10
  19.8 48.0 %all-gather.2.cloned.1.call-done = bf16[128,4,4096]{2,1,0:T(4,128)(2,1)} async-done(((bf16[4,4,4096]{2,1,0:T(4,128)(2,1)}), bf16[128,4,4096]{2,1,0:T(4,128)(2,1)}) %all-gather.2.cloned.1.call-update) | async-done | bytes 4194320 | tf_op jit(solution)/shard_map/all_gather | solution.py:73
  67.8 6.9 %reshape.47 = bf16[512,4096]{1,0:T(8,128)(2,1)} reshape(bf16[128,4,4096]{2,1,0:T(4,128)(2,1)} %all-gather.2.cloned.1.call-done) | data formatting | bytes 8388608 | tf_op jit(solution)/shard_map/reshape | solution.py:77
  74.7 0.0 copy-start.1
  74.7 0.0 copy-start.7
  74.7 4.3 fusion.31
  79.0 0.0 copy-done.1
  79.0 0.0 copy-done.7
  79.0 5.8 %convolution_add_fusion = f32[512,256]{1,0:T(8,128)S(1)} fusion(bf16[512,4096]{1,0:T(8,128)(2,1)S(1)} %copy-done.1, f32[4096,256]{1,0:T(8,128)} %param.16, f32[256]{0:T(256)S(1)} %copy-done.7), kind=kOutput, calls=%fused_computation.6 | convolution fusion | flops 6442582016 | bytes 8913920 | tf_op jit(solution)/shard_map/dot_general | solution.py:84
  84.9 0.0 copy-done
  84.9 8.7 %fusion.3 = f32[512,4096]{1,0:T(8,128)} fusion(bf16[224,4096]{1,0:T(8,128)(2,1)S(1)} %copy-done, bf16[512,4096]{1,0:T(8,128)(2,1)} %reshape.47, bf16[4096,224]{0,1:T(8,128)(2,1)} %param.14, f32[512,224]{0,1:T(8,128)S(1)} %fusion.31), kind=kOutput, calls=%fused_computation.8 | convolution fusion | flops 1879736320 | bytes 16711680 | tf_op jit(solution)/shard_map/dot_general | solution.py:82
  93.6 13.0 %convolution_subtract_fusion = f32[512,4096]{1,0:T(8,128)} fusion(f32[512,4096]{1,0:T(8,128)} %fusion.3, f32[256,4096]{1,0:T(8,128)} %param.19, f32[512,256]{1,0:T(8,128)S(1)} %convolution_add_fusion, f32[256]{0:T(256)S(1)} %exp.10), kind=kOutput, calls=%fused_computation.1 | convolution fusion | flops 6445334528 | bytes 21496832 | tf_op jit(solution)/shard_map/dot_general | solution.py:89
  106.6 0.0 copy-start.5
  106.6 0.0 copy-start.6
  106.6 0.0 all-reduce.2.cloned.1.call-update
  106.6 119.7 %all-reduce.2.cloned.1.call-done = f32[512,4096]{1,0:T(8,128)} async-done(((f32[512,4096]{1,0:T(8,128)}), f32[512,4096]{1,0:T(8,128)}) %all-reduce.2.cloned.1.call-update) | async-done | bytes 8388624 | tf_op jit(solution)/shard_map/psum | solution.py:90
  226.4 1.2 collective-permute-start
  227.6 0.0 copy-done.5
  227.6 0.0 copy-done.6
  227.6 0.1 fusion.18
  227.7 181.8 %all_to_all.20 = bf16[4,1,4]{2,1,0:T(2,128)(2,1)S(1)} all-to-all(bf16[4,1,4]{2,1,0:T(2,128)(2,1)S(1)} %copy.24), channel_id=1, replica_groups=mesh['expert'=4,'feat'=32] {'expert'}, dimensions={0} | all-to-all | bytes 64 | tf_op jit(solution)/shard_map/all_to_all | solution.py:70
  409.5 14.5 %all_to_all.21 = bf16[32,4,4]{2,1,0:T(4,128)(2,1)S(1)} all-to-all(bf16[32,4,4]{2,1,0:T(4,128)(2,1)S(1)} %stack.5), channel_id=1, replica_groups=mesh['expert'=4,'feat'=32] {'feat'}, dimensions={0} | all-to-all | bytes 2048 | tf_op jit(solution)/shard_map/all_to_all | solution.py:14
  424.1 0.1 mul.73
  424.2 0.1 mul.63
  424.3 0.0 copy-start.2
  424.3 0.0 collective-permute-done
  424.3 13.2 %multiply_reduce_fusion = (f32[256]{0:T(256)S(1)}, f32[256]{0:T(256)}, f32[512,256]{1,0:T(8,128)S(1)}) fusion(f32[512,256]{1,0:T(8,128)S(1)} %convolution_add_fusion, f32[512]{0:T(512)S(1)} %mul.73, f32[256]{0:T(256)S(1)} %exp.10, f32[256,4096]{1,0:T(8,128)} %param.19, f32[512,4096]{1,0:T(8,128)} %all-reduce.2.cloned.1.call-done, ...), kind=kOutput, calls=%fused_computation.9 | convolution fusion | flops 6448741888 | bytes 22027264 | tf_op jit(solution)/shard_map/dot_general | solution.py:94
  437.5 0.0 copy-done.2
  437.5 0.0 copy-start.4
  437.5 0.0 copy-start.3
  437.5 6.3 %fusion.29 = f32[4096,256]{1,0:T(8,128)} fusion(bf16[512,4096]{1,0:T(8,128)(2,1)S(1)} %copy-done.2, f32[512,256]{1,0:T(8,128)S(1)} %get-tuple-element.8, f32[512,256]{1,0:T(8,128)S(1)} %convolution_add_fusion, f32[256]{0:T(256)S(1)} %exp.10), kind=kOutput, calls=%fused_computation.42 | convolution fusion | flops 6443237376 | bytes 9438208 | tf_op jit(solution)/shard_map/dot_general | solution.py:48
  443.8 0.0 copy-done.4
  443.8 0.6 negate_multiply_fusion
  444.4 0.0 copy-done.3
  444.4 11.5 %fusion = f32[256,4096]{1,0:T(8,128)} fusion(f32[512,4096]{1,0:T(8,128)S(1)} %copy-done.3, f32[512,4096]{1,0:T(8,128)} %collective-permute-done, f32[512]{0:T(512)S(1)} %mul.63, f32[512,256]{1,0:T(8,128)S(1)} %convolution_add_fusion, f32[256]{0:T(256)S(1)} %exp.10), kind=kOutput, calls=%fused_computation.4 | convolution fusion | flops 6447431680 | bytes 21498880 | tf_op jit(solution)/shard_map/dot_general | solution.py:48
  (9 shorter events, 0.1 us)
Async XLA Ops:
  7.2 77.7 %copy-start = (bf16[224,4096]{1,0:T(8,128)(2,1)S(1)}, bf16[224,4096]{1,0:T(8,128)(2,1)}, u32[]{:S(2)}) copy-start(bf16[224,4096]{1,0:T(8,128)(2,1)} %param.15) | copy-start | bytes 5505028
  7.2 60.6 %all-gather.2.cloned.1.call-start = ((), (), s32[]{:S(2)}) async-start(), calls=%async_computation.3 | async-start | bytes 4325376 | tf_op jit(solution)/shard_map/all_gather | solution.py:73
  19.0 207.3 %all-reduce.2.cloned.1.call-start = ((), (), s32[]{:S(2)}) async-start(), calls=%async_computation.4 | async-start | bytes 16777216 | tf_op jit(solution)/shard_map/psum | solution.py:90
  74.7 4.4 copy-start.1
  74.7 4.4 copy-start.7
  106.6 121.0 %copy-start.5 = (s32[8,2]{0,1:T(2,128)S(1)}, s32[8,2]{0,1:T(2,128)}, u32[]{:S(2)}) copy-start(s32[8,2]{0,1:T(2,128)} %param.11) | copy-start | bytes 196
  106.6 121.0 %copy-start.6 = (bf16[8,2]{0,1:T(2,128)(2,1)S(1)}, bf16[8,2]{0,1:T(2,128)(2,1)}, u32[]{:S(2)}) copy-start(bf16[8,2]{0,1:T(2,128)(2,1)} %param.12) | copy-start | bytes 100
  226.4 197.9 %collective-permute-start = (f32[512,4096]{1,0:T(8,128)}, f32[512,4096]{1,0:T(8,128)}, u32[]{:S(2)}, u32[]{:S(2)}) collective-permute-start(f32[512,4096]{1,0:T(8,128)} %all-reduce.2.cloned.1.call-done), channel_id=1, source_target_pairs={{0,32},{32,0},{64,96},{96,64},{1,33},{33,1},{65,97},{97,65},{2,34}... | collective-permute-start | bytes 25165832 | tf_op jit(solution)/shard_map/ppermute | solution.py:24
  424.3 13.2 %copy-start.2 = (bf16[512,4096]{1,0:T(8,128)(2,1)S(1)}, bf16[512,4096]{1,0:T(8,128)(2,1)}, u32[]{:S(2)}) copy-start(bf16[512,4096]{1,0:T(8,128)(2,1)} %reshape.47) | copy-start | bytes 12582916
  437.5 6.3 %copy-start.4 = (f32[256]{0:T(256)S(1)}, f32[256]{0:T(256)}, u32[]{:S(2)}) copy-start(f32[256]{0:T(256)} %param.18) | copy-start | bytes 3076
  437.5 6.9 %copy-start.3 = (f32[512,4096]{1,0:T(8,128)S(1)}, f32[512,4096]{1,0:T(8,128)}, u32[]{:S(2)}) copy-start(f32[512,4096]{1,0:T(8,128)} %all-reduce.2.cloned.1.call-done) | copy-start | bytes 25165828
Sparse Core Ops, SparseCore 0:
  19.2 48.5 all-gather.1
  106.8 119.5 all-reduce.1
